TPU v7x, 32 devices: a whole 2x2x4 slice. The times are simulated.
32 devices in a mesh: groups: 2 (over y), node: 4 (over x, core), local: 4 (over z).
Axes of the slice: x: 2, y: 2, z: 4, core: 2. Of those that a mesh axis runs over, the one named last changes fastest.
Arguments:
- residual: bfloat16 [4, 512, 2048], P(None, ('groups', 'node', 'local')), parts along dimension 1, may hold values from -24 to 24
- query: bfloat16 [4, 512, 2048], P(None, ('groups', 'node', 'local')), parts along dimension 1, may hold values from -15 to 15
- new_keys: bfloat16 [4, 512, 256], P(None, ('groups', 'node', 'local')), parts along dimension 1, may hold values from -6 to 6
- new_values: bfloat16 [4, 512, 256], P(None, ('groups', 'node', 'local')), parts along dimension 1, may hold values from -6 to 6
- key_cache: bfloat16 [512, 80, 256], P(('groups', 'node', 'local')), parts along dimension 0, may hold values from -15 to 15
- value_cache: bfloat16 [512, 80, 256], P(('groups', 'node', 'local')), parts along dimension 0, may hold values from -6 to 6
- lengths: int32 [512], P(('groups', 'node', 'local')), parts along dimension 0, may hold values from 2 to 76
- norm_gain: float32 [2048], replicated, may hold values from 0.5 to 1.5
- expert_ids: int32 [4, 512, 8], P(None, ('groups', 'node', 'local')), parts along dimension 1, may hold values from 0 to 15, all different within a row; in each aligned block of 16 rows (0 to 15, 16 to 31, ..., all dimensions but the last counted through in order) at most 16 rows name the same one
- gate_scores: float32 [4, 512, 8], P(None, ('groups', 'node', 'local')), parts along dimension 1, may hold values from 0.05 to 1
- learner_gate: float32 [16, 2048, 384], P(None, ('node', 'local')), may hold values from -0.125 to 0.125
- learner_up: float32 [16, 2048, 384], P(None, ('node', 'local')), may hold values from -0.125 to 0.125
- learner_down: float32 [16, 2048, 384], P(None, ('node', 'local')), may hold values from -0.625 to 0.625
Outputs:
- mixture: bfloat16 [4, 512, 2048], P(None, ('groups', 'node', 'local')), parts along dimension 1
- stream: bfloat16 [4, 512, 2048], P(None, ('groups', 'node', 'local')), parts along dimension 1
There are 2 independent parts, one for each index of `groups`. A program takes and returns all parts, laid end to end along the dimension named above; an argument that names none is the same for every part. Nothing has to cross between parts.
Inputs may be any that keep to these rules, and one draw needn't show every extreme that they name: `expert_ids`: each row names 8 different experts; in one step, no expert is named by more than 16 of the 16 rows that one device holds.
All inputs are finite; a program needn't handle non-finite values.
Results may differ from a plain program's by a relative error of at most 0.0087.
Values may be sent and summed in bfloat16 or wider, within the bound.
A program may use at most 128 MiB of HBM per device.

v0:
```python
import math

import jax
import jax.numpy as jnp
from jax import lax
from jax.sharding import PartitionSpec as P

HEADS = 16
KV_HEADS = 2
HEAD_DIM = 128


epsilon = 1e-06


def place_rows(expert_list, expert_count, capacity):
    targets = jnp.arange(expert_count, dtype=jnp.int32)
    matches = (expert_list[:, :, None] == targets).astype(jnp.int32)
    counts = jnp.sum(matches, axis=1, dtype=jnp.int32)
    earlier = jnp.cumsum(counts, axis=0, dtype=jnp.int32) - counts
    ranked = jnp.sum(matches * earlier[:, None, :], axis=2, dtype=jnp.int32)
    return jnp.where(expert_list >= 0, expert_list * capacity + ranked, -1)


def pick_matrix(slot_map, slot_total):
    positions = jnp.arange(slot_total, dtype=jnp.int32)
    hits = (slot_map[None, :, :] == positions[:, None, None]).astype(jnp.int32)
    return jnp.sum(hits, axis=2, dtype=jnp.int32).astype(jnp.bfloat16)


def expert_rows(blocks, gate_w, up_w, down_w):
    gate_part = jnp.einsum("sjcd,jdf->sjcf", blocks, gate_w, preferred_element_type=jnp.float32)
    up_part = jnp.einsum("sjcd,jdf->sjcf", blocks, up_w, preferred_element_type=jnp.float32)
    active = (jax.nn.silu(gate_part) * up_part).astype(jnp.bfloat16)
    result = jnp.einsum("sjcf,jdf->sjcd", active, down_w, preferred_element_type=jnp.float32)
    return result.astype(jnp.bfloat16)


def attend(query_now, key_cache, value_cache, new_keys, new_values, lengths, step_index):
    row_count = query_now.shape[0]
    group_size = HEADS // KV_HEADS
    queries = query_now.reshape(row_count, KV_HEADS, group_size, HEAD_DIM)
    cache_keys = key_cache.reshape(row_count, key_cache.shape[1], KV_HEADS, HEAD_DIM)
    cache_values = value_cache.reshape(row_count, value_cache.shape[1], KV_HEADS, HEAD_DIM)
    fresh_keys = jnp.transpose(new_keys, (1, 0, 2)).reshape(
        row_count, new_keys.shape[0], KV_HEADS, HEAD_DIM
    )
    fresh_values = jnp.transpose(new_values, (1, 0, 2)).reshape(
        row_count, new_values.shape[0], KV_HEADS, HEAD_DIM
    )
    score_scale = 1.0 / math.sqrt(HEAD_DIM)
    cache_scores = (
        jnp.einsum("rgqd,rcgd->rgqc", queries, cache_keys, preferred_element_type=jnp.float32)
        * score_scale
    )
    fresh_scores = (
        jnp.einsum("rgqd,rjgd->rgqj", queries, fresh_keys, preferred_element_type=jnp.float32)
        * score_scale
    )
    positions = jnp.arange(key_cache.shape[1], dtype=jnp.int32)
    cache_live = positions[None, :] < lengths[:, None]
    fresh_live = jnp.arange(new_keys.shape[0], dtype=jnp.int32) <= step_index
    cache_scores = jnp.where(cache_live[:, None, None, :], cache_scores, -1e30)
    fresh_scores = jnp.where(fresh_live[None, None, None, :], fresh_scores, -1e30)
    highest = jnp.maximum(jnp.max(cache_scores, axis=-1), jnp.max(fresh_scores, axis=-1))[..., None]
    cache_exp = jnp.exp(cache_scores - highest)
    fresh_exp = jnp.exp(fresh_scores - highest)
    denominator = jnp.sum(cache_exp, axis=-1, keepdims=True) + jnp.sum(
        fresh_exp, axis=-1, keepdims=True
    )
    cache_probs = (cache_exp / denominator).astype(jnp.bfloat16)
    fresh_probs = (fresh_exp / denominator).astype(jnp.bfloat16)
    attended = jnp.einsum(
        "rgqc,rcgd->rgqd", cache_probs, cache_values, preferred_element_type=jnp.float32
    )
    attended = attended + jnp.einsum(
        "rgqj,rjgd->rgqd", fresh_probs, fresh_values, preferred_element_type=jnp.float32
    )
    return attended.reshape(row_count, HEADS * HEAD_DIM)


def body(
    residual,
    query,
    new_keys,
    new_values,
    key_cache,
    value_cache,
    lengths,
    norm_gain,
    expert_ids,
    gate_scores,
    learner_gate,
    learner_up,
    learner_down,
):
    gate_half = learner_gate.astype(jnp.bfloat16)
    up_half = learner_up.astype(jnp.bfloat16)
    down_half = learner_down.astype(jnp.bfloat16)
    owned_gate, owned_up, owned_down = (
        lax.all_to_all(gate_half, ("node", "local"), split_axis=0, concat_axis=1, tiled=True),
        lax.all_to_all(up_half, ("node", "local"), split_axis=0, concat_axis=1, tiled=True),
        lax.all_to_all(down_half, ("node", "local"), split_axis=0, concat_axis=1, tiled=True),
    )
    row_count = residual.shape[1]
    model_width = residual.shape[2]
    top_count = expert_ids.shape[2]
    expert_total = learner_gate.shape[0]
    owned_count = owned_gate.shape[0]
    capacity = max(2, 2 * row_count * top_count // expert_total)
    mixtures = []
    streams = []
    for step_index in range(residual.shape[0]):
        attended = attend(
            query[step_index], key_cache, value_cache, new_keys, new_values, lengths, step_index
        )
        hidden_state = residual[step_index].astype(jnp.float32) + attended
        mean_square = jnp.mean(hidden_state * hidden_state, axis=-1, keepdims=True)
        normed = (hidden_state * lax.rsqrt(mean_square + epsilon) * norm_gain).astype(jnp.bfloat16)
        step_ids = expert_ids[step_index]
        weights = gate_scores[step_index] / jnp.sum(gate_scores[step_index], axis=-1, keepdims=True)
        slot_map = place_rows(step_ids, expert_total, capacity)
        picker = pick_matrix(slot_map, expert_total * capacity)
        outgoing = jnp.dot(picker, normed, preferred_element_type=jnp.float32).astype(jnp.bfloat16)
        outgoing = outgoing.reshape(expert_total, capacity, model_width)
        incoming = lax.all_to_all(
            outgoing, ("node", "local"), split_axis=0, concat_axis=0, tiled=True
        )
        sources = incoming.shape[0] // owned_count
        blocks = incoming.reshape(sources, owned_count, incoming.shape[1], model_width)
        served = expert_rows(blocks, owned_gate, owned_up, owned_down).reshape(incoming.shape)
        returned = lax.all_to_all(
            served, ("node", "local"), split_axis=0, concat_axis=0, tiled=True
        )
        flat_rows = returned.reshape(expert_total * capacity, model_width)
        picked = flat_rows[slot_map]
        mixture_sum = jnp.sum(weights[:, :, None] * picked.astype(jnp.float32), axis=1)
        mixtures.append(mixture_sum.astype(jnp.bfloat16))
        streams.append((hidden_state + mixture_sum).astype(jnp.bfloat16))
    return (jnp.stack(mixtures), jnp.stack(streams))


def solution(mesh):
    return jax.shard_map(
        body,
        mesh=mesh,
        in_specs=(
            P(None, ("groups", "node", "local"), None),
            P(None, ("groups", "node", "local"), None),
            P(None, ("groups", "node", "local"), None),
            P(None, ("groups", "node", "local"), None),
            P(("groups", "node", "local"), None, None),
            P(("groups", "node", "local"), None, None),
            P(("groups", "node", "local")),
            P(),
            P(None, ("groups", "node", "local"), None),
            P(None, ("groups", "node", "local"), None),
            P(None, ("node", "local"), None),
            P(None, ("node", "local"), None),
            P(None, ("node", "local"), None),
        ),
        out_specs=(
            P(None, ("groups", "node", "local"), None),
            P(None, ("groups", "node", "local"), None),
        ),
        check_vma=False,
    )
```

profile of v0, /device:TPU:0, one launch (start us, length us, event | category | flops | bytes accessed | tf_op | source)
XLA Modules:
  0.0 391.3 jit_solution(7870467450626337806)
XLA Ops:
  0.7 1.1 convert_bitcast_fusion.6
  1.8 1.6 slice_bitcast_fusion.3
  8.4 1.5 convolution_convert_fusion.4
  9.9 7.4 %all-to-all-start.9 = ((bf16[16,16,2048]{2,1,0:T(8,128)(2,1)}), bf16[16,16,2048]{2,1,0:T(8,128)(2,1)S(1)}, u32[]{:S(2)}, u32[]{:S(2)}) async-start(bf16[16,16,2048]{2,1,0:T(8,128)(2,1)} %bitcast.445), calls=%async_computation.9 | async-start | bytes 2097152 | tf_op jit(solution)/shard_map/all_to_all | solution.py:126
  21.3 1.5 convolution_convert_fusion.5
  22.7 21.5 %all-to-all-done.9 = bf16[16,16,2048]{2,1,0:T(8,128)(2,1)S(1)} async-done(((bf16[16,16,2048]{2,1,0:T(8,128)(2,1)}), bf16[16,16,2048]{2,1,0:T(8,128)(2,1)S(1)}, u32[]{:S(2)}, u32[]{:S(2)}) %all-to-all-start.9) | async-done | bytes 1048608 | tf_op jit(solution)/shard_map/all_to_all | solution.py:126
  44.2 4.3 %all-to-all-start.7 = ((bf16[16,16,2048]{2,1,0:T(8,128)(2,1)}), bf16[16,16,2048]{2,1,0:T(8,128)(2,1)}, u32[]{:S(2)}, u32[]{:S(2)}) async-start(bf16[16,16,2048]{2,1,0:T(8,128)(2,1)} %bitcast.446), calls=%async_computation.7 | async-start | bytes 2097152 | tf_op jit(solution)/shard_map/all_to_all | solution.py:126
  50.6 1.5 convolution_convert_fusion.6
  52.1 23.4 %all-to-all-done.7 = bf16[16,16,2048]{2,1,0:T(8,128)(2,1)} async-done(((bf16[16,16,2048]{2,1,0:T(8,128)(2,1)}), bf16[16,16,2048]{2,1,0:T(8,128)(2,1)}, u32[]{:S(2)}, u32[]{:S(2)}) %all-to-all-start.7) | async-done | bytes 1048608 | tf_op jit(solution)/shard_map/all_to_all | solution.py:126
  75.5 3.7 all-to-all-start.5
  79.2 3.3 convert_element_type.271
  82.5 23.6 %all-to-all-done.5 = bf16[16,16,2048]{2,1,0:T(8,128)(2,1)S(1)} async-done(((bf16[16,16,2048]{2,1,0:T(8,128)(2,1)}), bf16[16,16,2048]{2,1,0:T(8,128)(2,1)S(1)}, u32[]{:S(2)}, u32[]{:S(2)}) %all-to-all-start.5) | async-done | bytes 1048608 | tf_op jit(solution)/shard_map/all_to_all | solution.py:126
  106.1 4.4 %all-to-all-start.3 = ((bf16[16,128,384]{2,1,0:T(8,128)(2,1)}), bf16[16,128,384]{2,1,0:T(8,128)(2,1)}, u32[]{:S(2)}, u32[]{:S(2)}) async-start(bf16[16,128,384]{2,1,0:T(8,128)(2,1)} %convert_element_type.271), calls=%async_computation.3 | async-start | bytes 3145728 | tf_op jit(solution)/shard_map/all_to_all | solution.py:103
  110.5 3.3 convert_element_type.269
  113.8 34.9 %all-to-all-done.3 = bf16[16,128,384]{2,1,0:T(8,128)(2,1)} async-done(((bf16[16,128,384]{2,1,0:T(8,128)(2,1)}), bf16[16,128,384]{2,1,0:T(8,128)(2,1)}, u32[]{:S(2)}, u32[]{:S(2)}) %all-to-all-start.3) | async-done | bytes 1572896 | tf_op jit(solution)/shard_map/all_to_all | solution.py:103
  148.7 4.4 %all-to-all-start.2 = ((bf16[16,128,384]{2,1,0:T(8,128)(2,1)}), bf16[16,128,384]{2,1,0:T(8,128)(2,1)}, u32[]{:S(2)}, u32[]{:S(2)}) async-start(bf16[16,128,384]{2,1,0:T(8,128)(2,1)} %convert_element_type.269), calls=%async_computation.2 | async-start | bytes 3145728 | tf_op jit(solution)/shard_map/all_to_all | solution.py:102
  153.1 3.3 convert_element_type.268
  156.4 34.9 %all-to-all-done.2 = bf16[16,128,384]{2,1,0:T(8,128)(2,1)} async-done(((bf16[16,128,384]{2,1,0:T(8,128)(2,1)}), bf16[16,128,384]{2,1,0:T(8,128)(2,1)}, u32[]{:S(2)}, u32[]{:S(2)}) %all-to-all-start.2) | async-done | bytes 1572896 | tf_op jit(solution)/shard_map/all_to_all | solution.py:102
  191.3 3.7 all-to-all-start.1
  197.0 1.0 fusion.120
  199.1 1.5 convolution_convert_fusion.7
  200.6 32.6 %all-to-all-done.1 = bf16[16,128,384]{2,1,0:T(8,128)(2,1)S(1)} async-done(((bf16[16,128,384]{2,1,0:T(8,128)(2,1)}), bf16[16,128,384]{2,1,0:T(8,128)(2,1)S(1)}, u32[]{:S(2)}, u32[]{:S(2)}) %all-to-all-start.1) | async-done | bytes 1572896 | tf_op jit(solution)/shard_map/all_to_all | solution.py:101
  233.2 4.3 %all-to-all-start = ((bf16[16,16,2048]{2,1,0:T(8,128)(2,1)}), bf16[16,16,2048]{2,1,0:T(8,128)(2,1)}, u32[]{:S(2)}, u32[]{:S(2)}) async-start(bf16[16,16,2048]{2,1,0:T(8,128)(2,1)} %bitcast.447), calls=%async_computation | async-start | bytes 2097152 | tf_op jit(solution)/shard_map/all_to_all | solution.py:126
  237.5 1.5 convolution_bitcast_fusion.1
  239.0 4.3 %convolution_convert_fusion = bf16[16,16,2048]{2,1,0:T(8,128)(2,1)} fusion(bf16[2048,384,1]{1,0,2:T(8,128)(2,1)} %bitcast.22, bf16[16,16,2048]{2,1,0:T(8,128)(2,1)S(1)} %copy-done.3, bf16[2048,384,1]{1,0,2:T(8,128)(2,1)} %bitcast.16, f32[16,1,16,384]{3,2,0,1:T(8,128)} %convolution_bitcast_fusion.1), kind=kOutput, calls=%fused_computation.4 | convolution fusion | flops 806420480 | bytes 5636096 | tf_op jit(solution)/shard_map/sjcf,jdf->sjcd/dot_general | solution.py:35
  243.3 21.1 %all-to-all-done = bf16[16,16,2048]{2,1,0:T(8,128)(2,1)} async-done(((bf16[16,16,2048]{2,1,0:T(8,128)(2,1)}), bf16[16,16,2048]{2,1,0:T(8,128)(2,1)}, u32[]{:S(2)}, u32[]{:S(2)}) %all-to-all-start) | async-done | bytes 1048608 | tf_op jit(solution)/shard_map/all_to_all | solution.py:126
  264.5 3.8 all-to-all-start.10
  268.3 2.7 convolution_bitcast_fusion.3
  271.1 4.6 %convolution_convert_fusion.1 = bf16[16,16,2048]{2,1,0:T(8,128)(2,1)} fusion(bf16[2048,384,1]{1,0,2:T(8,128)(2,1)} %bitcast.22, bf16[16,16,2048]{2,1,0:T(8,128)(2,1)} %all-to-all-done.7, bf16[2048,384,1]{1,0,2:T(8,128)(2,1)} %bitcast.16, f32[16,1,16,384]{3,2,0,1:T(8,128)} %convolution_bitcast_fusion.3), kind=kOutput, calls=%fused_computation.5 | convolution fusion | flops 806420480 | bytes 5636096 | tf_op jit(solution)/shard_map/sjcf,jdf->sjcd/dot_general | solution.py:35
  275.7 19.4 %all-to-all-done.10 = bf16[16,16,2048]{2,1,0:T(8,128)(2,1)S(1)} async-done(((bf16[16,16,2048]{2,1,0:T(8,128)(2,1)}), bf16[16,16,2048]{2,1,0:T(8,128)(2,1)S(1)}, u32[]{:S(2)}, u32[]{:S(2)}) %all-to-all-start.10) | async-done | bytes 1048608 | tf_op jit(solution)/shard_map/all_to_all | solution.py:132
  295.1 4.3 %all-to-all-start.8 = ((bf16[16,16,2048]{2,1,0:T(8,128)(2,1)}), bf16[16,16,2048]{2,1,0:T(8,128)(2,1)}, u32[]{:S(2)}, u32[]{:S(2)}) async-start(bf16[16,16,2048]{2,1,0:T(8,128)(2,1)} %convolution_convert_fusion.1), calls=%async_computation.8 | async-start | bytes 2097152 | tf_op jit(solution)/shard_map/all_to_all | solution.py:132
  299.4 2.7 convolution_bitcast_fusion.5
  302.1 4.6 %convolution_convert_fusion.2 = bf16[16,16,2048]{2,1,0:T(8,128)(2,1)} fusion(bf16[2048,384,1]{1,0,2:T(8,128)(2,1)} %bitcast.22, bf16[16,16,2048]{2,1,0:T(8,128)(2,1)} %copy-done.4, bf16[2048,384,1]{1,0,2:T(8,128)(2,1)} %bitcast.16, f32[16,1,16,384]{3,2,0,1:T(8,128)} %convolution_bitcast_fusion.5), kind=kOutput, calls=%fused_computation.6 | convolution fusion | flops 806420480 | bytes 5636096 | tf_op jit(solution)/shard_map/sjcf,jdf->sjcd/dot_general | solution.py:35
  306.8 19.6 %all-to-all-done.8 = bf16[16,16,2048]{2,1,0:T(8,128)(2,1)} async-done(((bf16[16,16,2048]{2,1,0:T(8,128)(2,1)}), bf16[16,16,2048]{2,1,0:T(8,128)(2,1)}, u32[]{:S(2)}, u32[]{:S(2)}) %all-to-all-start.8) | async-done | bytes 1048608 | tf_op jit(solution)/shard_map/all_to_all | solution.py:132
  326.4 4.3 %all-to-all-start.6 = ((bf16[16,16,2048]{2,1,0:T(8,128)(2,1)}), bf16[16,16,2048]{2,1,0:T(8,128)(2,1)}, u32[]{:S(2)}, u32[]{:S(2)}) async-start(bf16[16,16,2048]{2,1,0:T(8,128)(2,1)} %convolution_convert_fusion.2), calls=%async_computation.6 | async-start | bytes 2097152 | tf_op jit(solution)/shard_map/all_to_all | solution.py:132
  330.7 2.7 convolution_bitcast_fusion.7
  333.4 4.6 %convolution_convert_fusion.3 = bf16[16,16,2048]{2,1,0:T(8,128)(2,1)} fusion(bf16[2048,384,1]{1,0,2:T(8,128)(2,1)} %bitcast.22, bf16[16,16,2048]{2,1,0:T(8,128)(2,1)} %all-to-all-done, bf16[2048,384,1]{1,0,2:T(8,128)(2,1)} %bitcast.16, f32[16,1,16,384]{3,2,0,1:T(8,128)} %convolution_bitcast_fusion.7), kind=kOutput, calls=%fused_computation.7 | convolution fusion | flops 806420480 | bytes 5636096 | tf_op jit(solution)/shard_map/sjcf,jdf->sjcd/dot_general | solution.py:35
  338.1 19.6 %all-to-all-done.6 = bf16[16,16,2048]{2,1,0:T(8,128)(2,1)} async-done(((bf16[16,16,2048]{2,1,0:T(8,128)(2,1)}), bf16[16,16,2048]{2,1,0:T(8,128)(2,1)}, u32[]{:S(2)}, u32[]{:S(2)}) %all-to-all-start.6) | async-done | bytes 1048608 | tf_op jit(solution)/shard_map/all_to_all | solution.py:132
  357.7 3.7 all-to-all-start.4
  365.6 0.8 copy.108
  367.2 0.8 copy.98
  370.2 0.9 gather_fusion.3
  371.2 2.8 gather_fusion.2
  374.0 2.8 gather_fusion.1
  377.3 1.2 fusion.21
  378.5 1.2 fusion.22
  379.7 8.5 %all-to-all-done.4 = bf16[16,16,2048]{2,1,0:T(8,128)(2,1)S(1)} async-done(((bf16[16,16,2048]{2,1,0:T(8,128)(2,1)}), bf16[16,16,2048]{2,1,0:T(8,128)(2,1)S(1)}, u32[]{:S(2)}, u32[]{:S(2)}) %all-to-all-start.4) | async-done | bytes 1048608 | tf_op jit(solution)/shard_map/all_to_all | solution.py:132
  388.3 0.9 gather_fusion
  (186 shorter events, 23.7 us)
Async XLA Ops:
  0.6 4.3 %copy-start = (bf16[16,80,256]{2,1,0:T(8,128)(2,1)S(1)}, bf16[16,80,256]{2,1,0:T(8,128)(2,1)}, u32[]{:S(2)}) copy-start(bf16[16,80,256]{2,1,0:T(8,128)(2,1)} %param.18) | copy-start | bytes 1966084
  0.6 2.7 copy-start.28
  0.7 2.8 copy-start.35
  0.7 3.1 copy-start.1
  0.7 3.9 copy-start.29
  3.4 45.3 %copy-start.31 = (bf16[16,4,2,128]{3,2,0,1:T(2,128)(2,1)}, bf16[16,4,2,128]{3,2,0,1:T(2,128)(2,1)S(1)}, u32[]{:S(2)}) copy-start(bf16[16,4,2,128]{3,2,0,1:T(2,128)(2,1)S(1)} %reshape.622) | copy-start | bytes 98308
  4.3 1.1 copy-start.23
  4.6 45.3 %copy-start.30 = (bf16[16,4,2,128]{3,2,0,1:T(2,128)(2,1)}, bf16[16,4,2,128]{3,2,0,1:T(2,128)(2,1)S(1)}, u32[]{:S(2)}) copy-start(bf16[16,4,2,128]{3,2,0,1:T(2,128)(2,1)S(1)} %reshape.624) | copy-start | bytes 98308
  4.6 3.7 copy-start.5
  4.6 3.7 copy-start.24
  5.4 4.5 %copy-start.10 = (f32[16,2,8,128]{3,2,1,0:T(8,128)}, f32[16,2,8,128]{3,2,1,0:T(8,128)S(1)}, u32[]{:S(2)}) copy-start(f32[16,2,8,128]{3,2,1,0:T(8,128)S(1)} %get-tuple-element.46) | copy-start | bytes 393220
  9.9 34.3 %all-to-all-start.9 = ((bf16[16,16,2048]{2,1,0:T(8,128)(2,1)}), bf16[16,16,2048]{2,1,0:T(8,128)(2,1)S(1)}, u32[]{:S(2)}, u32[]{:S(2)}) async-start(bf16[16,16,2048]{2,1,0:T(8,128)(2,1)} %bitcast.445), calls=%async_computation.9 | async-start | bytes 2097152 | tf_op jit(solution)/shard_map/all_to_all | solution.py:126
  18.7 1.4 copy-start.25
  20.6 23.6 %copy-start.12 = (f32[16,2,8,128]{3,2,1,0:T(8,128)}, f32[16,2,8,128]{3,2,1,0:T(8,128)S(1)}, u32[]{:S(2)}) copy-start(f32[16,2,8,128]{3,2,1,0:T(8,128)S(1)} %get-tuple-element.52) | copy-start | bytes 393220
  44.2 5.2 %copy-start.2 = (bf16[16,16,2048]{2,1,0:T(8,128)(2,1)}, bf16[16,16,2048]{2,1,0:T(8,128)(2,1)S(1)}, u32[]{:S(2)}) copy-start(bf16[16,16,2048]{2,1,0:T(8,128)(2,1)S(1)} %all-to-all-done.9) | copy-start | bytes 3145732
  44.2 31.3 %all-to-all-start.7 = ((bf16[16,16,2048]{2,1,0:T(8,128)(2,1)}), bf16[16,16,2048]{2,1,0:T(8,128)(2,1)}, u32[]{:S(2)}, u32[]{:S(2)}) async-start(bf16[16,16,2048]{2,1,0:T(8,128)(2,1)} %bitcast.446), calls=%async_computation.7 | async-start | bytes 2097152 | tf_op jit(solution)/shard_map/all_to_all | solution.py:126
  50.6 24.9 %copy-start.14 = (f32[16,2,8,128]{3,2,1,0:T(8,128)}, f32[16,2,8,128]{3,2,1,0:T(8,128)S(1)}, u32[]{:S(2)}) copy-start(f32[16,2,8,128]{3,2,1,0:T(8,128)S(1)} %get-tuple-element.58) | copy-start | bytes 393220
  75.5 30.6 %all-to-all-start.5 = ((bf16[16,16,2048]{2,1,0:T(8,128)(2,1)}), bf16[16,16,2048]{2,1,0:T(8,128)(2,1)S(1)}, u32[]{:S(2)}, u32[]{:S(2)}) async-start(bf16[16,16,2048]{2,1,0:T(8,128)(2,1)} %bitcast.448), calls=%async_computation.5 | async-start | bytes 2097152 | tf_op jit(solution)/shard_map/all_to_all | solution.py:126
  106.1 42.6 %copy-start.4 = (bf16[16,16,2048]{2,1,0:T(8,128)(2,1)}, bf16[16,16,2048]{2,1,0:T(8,128)(2,1)S(1)}, u32[]{:S(2)}) copy-start(bf16[16,16,2048]{2,1,0:T(8,128)(2,1)S(1)} %all-to-all-done.5) | copy-start | bytes 3145732
  106.1 42.6 %all-to-all-start.3 = ((bf16[16,128,384]{2,1,0:T(8,128)(2,1)}), bf16[16,128,384]{2,1,0:T(8,128)(2,1)}, u32[]{:S(2)}, u32[]{:S(2)}) async-start(bf16[16,128,384]{2,1,0:T(8,128)(2,1)} %convert_element_type.271), calls=%async_computation.3 | async-start | bytes 3145728 | tf_op jit(solution)/shard_map/all_to_all | solution.py:103
  148.7 42.6 %all-to-all-start.2 = ((bf16[16,128,384]{2,1,0:T(8,128)(2,1)}), bf16[16,128,384]{2,1,0:T(8,128)(2,1)}, u32[]{:S(2)}, u32[]{:S(2)}) async-start(bf16[16,128,384]{2,1,0:T(8,128)(2,1)} %convert_element_type.269), calls=%async_computation.2 | async-start | bytes 3145728 | tf_op jit(solution)/shard_map/all_to_all | solution.py:102
  156.4 39.3 %copy-start.22 = (bf16[2,8,16,128]{3,1,2,0:T(8,128)(2,1)S(1)}, bf16[2,8,16,128]{3,1,2,0:T(8,128)(2,1)}, u32[]{:S(2)}) copy-start(bf16[2,8,16,128]{3,1,2,0:T(8,128)(2,1)} %get-tuple-element.22) | copy-start | bytes 196612
  156.4 39.4 %copy-start.32 = (bf16[16,4,2,128]{3,2,0,1:T(2,128)(2,1)S(1)}, bf16[16,4,2,128]{3,2,0,1:T(2,128)(2,1)}, u32[]{:S(2)}) copy-start(bf16[16,4,2,128]{3,2,0,1:T(2,128)(2,1)} %copy-done.31) | copy-start | bytes 98308
  191.3 41.9 %all-to-all-start.1 = ((bf16[16,128,384]{2,1,0:T(8,128)(2,1)}), bf16[16,128,384]{2,1,0:T(8,128)(2,1)S(1)}, u32[]{:S(2)}, u32[]{:S(2)}) async-start(bf16[16,128,384]{2,1,0:T(8,128)(2,1)} %convert_element_type.268), calls=%async_computation.1 | async-start | bytes 3145728 | tf_op jit(solution)/shard_map/all_to_all | solution.py:101
  195.7 2.3 copy-start.26
  198.5 0.7 copy-start.20
  199.1 38.4 %copy-start.3 = (bf16[16,16,2048]{2,1,0:T(8,128)(2,1)S(1)}, bf16[16,16,2048]{2,1,0:T(8,128)(2,1)}, u32[]{:S(2)}) copy-start(bf16[16,16,2048]{2,1,0:T(8,128)(2,1)} %copy-done.2) | copy-start | bytes 3145732
  233.2 31.3 %all-to-all-start = ((bf16[16,16,2048]{2,1,0:T(8,128)(2,1)}), bf16[16,16,2048]{2,1,0:T(8,128)(2,1)}, u32[]{:S(2)}, u32[]{:S(2)}) async-start(bf16[16,16,2048]{2,1,0:T(8,128)(2,1)} %bitcast.447), calls=%async_computation | async-start | bytes 2097152 | tf_op jit(solution)/shard_map/all_to_all | solution.py:126
  264.5 30.6 %all-to-all-start.10 = ((bf16[16,16,2048]{2,1,0:T(8,128)(2,1)}), bf16[16,16,2048]{2,1,0:T(8,128)(2,1)S(1)}, u32[]{:S(2)}, u32[]{:S(2)}) async-start(bf16[16,16,2048]{2,1,0:T(8,128)(2,1)} %convolution_convert_fusion), calls=%async_computation.10 | async-start | bytes 2097152 | tf_op jit(solution)/shard_map/all_to_all | solution.py:132
  295.1 31.3 %all-to-all-start.8 = ((bf16[16,16,2048]{2,1,0:T(8,128)(2,1)}), bf16[16,16,2048]{2,1,0:T(8,128)(2,1)}, u32[]{:S(2)}, u32[]{:S(2)}) async-start(bf16[16,16,2048]{2,1,0:T(8,128)(2,1)} %convolution_convert_fusion.1), calls=%async_computation.8 | async-start | bytes 2097152 | tf_op jit(solution)/shard_map/all_to_all | solution.py:132
  326.4 31.3 %all-to-all-start.6 = ((bf16[16,16,2048]{2,1,0:T(8,128)(2,1)}), bf16[16,16,2048]{2,1,0:T(8,128)(2,1)}, u32[]{:S(2)}, u32[]{:S(2)}) async-start(bf16[16,16,2048]{2,1,0:T(8,128)(2,1)} %convolution_convert_fusion.2), calls=%async_computation.6 | async-start | bytes 2097152 | tf_op jit(solution)/shard_map/all_to_all | solution.py:132
  338.1 23.3 %copy-start.21 = (f32[16,2,8,128]{3,2,1,0:T(8,128)S(1)}, f32[16,2,8,128]{3,2,1,0:T(8,128)}, u32[]{:S(2)}) copy-start(f32[16,2,8,128]{3,2,1,0:T(8,128)} %copy-done.20) | copy-start | bytes 393220
  338.1 24.0 %copy-start.15 = (f32[16,2,8,128]{3,2,1,0:T(8,128)S(1)}, f32[16,2,8,128]{3,2,1,0:T(8,128)}, u32[]{:S(2)}) copy-start(f32[16,2,8,128]{3,2,1,0:T(8,128)} %copy-done.14) | copy-start | bytes 393220
  338.1 24.6 %copy-start.13 = (f32[16,2,8,128]{3,2,1,0:T(8,128)S(1)}, f32[16,2,8,128]{3,2,1,0:T(8,128)}, u32[]{:S(2)}) copy-start(f32[16,2,8,128]{3,2,1,0:T(8,128)} %copy-done.12) | copy-start | bytes 393220
  338.1 25.3 %copy-start.11 = (f32[16,2,8,128]{3,2,1,0:T(8,128)S(1)}, f32[16,2,8,128]{3,2,1,0:T(8,128)}, u32[]{:S(2)}) copy-start(f32[16,2,8,128]{3,2,1,0:T(8,128)} %copy-done.10) | copy-start | bytes 393220
  338.1 26.8 %copy-start.27 = (f32[4,16,8]{1,2,0:T(8,128)S(1)}, f32[4,16,8]{1,2,0:T(8,128)}, u32[]{:S(2)}) copy-start(f32[4,16,8]{1,2,0:T(8,128)} %param.22) | copy-start | bytes 6148
  357.7 30.6 %all-to-all-start.4 = ((bf16[16,16,2048]{2,1,0:T(8,128)(2,1)}), bf16[16,16,2048]{2,1,0:T(8,128)(2,1)S(1)}, u32[]{:S(2)}, u32[]{:S(2)}) async-start(bf16[16,16,2048]{2,1,0:T(8,128)(2,1)} %convolution_convert_fusion.3), calls=%async_computation.4 | async-start | bytes 2097152 | tf_op jit(solution)/shard_map/all_to_all | solution.py:132
  374.0 2.8 copy-start.33
  377.3 2.4 copy-start.6
  378.5 9.8 %copy-start.8 = (f32[16,2048]{1,0:T(8,128)}, f32[16,2048]{1,0:T(8,128)S(1)}, u32[]{:S(2)}) copy-start(f32[16,2048]{1,0:T(8,128)S(1)} %fusion.21) | copy-start | bytes 393220
  388.3 0.9 copy-start.34
  389.2 1.3 copy-start.7
  389.2 1.3 copy-start.9
  389.2 1.3 copy-start.16
  389.2 1.3 copy-start.17
  389.3 1.2 copy-start.18
  389.3 1.2 copy-start.19
where the time goes:
time: 393 us; the launch traced here: 391 us
  waiting for transfers between devices  259 us (66%)
  starting transfers between devices  48.3 us (12%)
  matrix products  40.2 us (10%)
  other arithmetic  21.2 us (5%)
  local copies, waits for them, and re-layouts  21 us (5%)
    all_to_all x4, waiting for transfers between devices, body(): lax.all_to_all(outgoing, ('node', 'local'), split_axis=0, concat_axis=0,...  89.7 us
    all_to_all x4, waiting for transfers between devices, body(): lax.all_to_all(served, ('node', 'local'), split_axis=0, concat_axis=0, ti...  67.1 us
    all_to_all x1, waiting for transfers between devices, body(): lax.all_to_all(up_half, ('node', 'local'), split_axis=0, concat_axis=1, t...  34.9 us
    all_to_all x1, waiting for transfers between devices, body(): lax.all_to_all(down_half, ('node', 'local'), split_axis=0, concat_axis=1,...  34.9 us
    all_to_all x1, waiting for transfers between devices, body(): lax.all_to_all(gate_half, ('node', 'local'), split_axis=0, concat_axis=1,...  32.6 us
    all_to_all x4, starting transfers between devices, body(): lax.all_to_all(outgoing, ('node', 'local'), split_axis=0, concat_axis=0,...  19.7 us
    dot_general x4, matrix products, expert_rows(): jnp.einsum('sjcf,jdf->sjcd', active, down_w, preferred_element_type=jnp.f...  18.2 us
    all_to_all x4, starting transfers between devices, body(): lax.all_to_all(served, ('node', 'local'), split_axis=0, concat_axis=0, ti...  16.2 us
  transfers between devices with their start and end apart: 11, of which 11 were waited for; matrix products, arithmetic and copies ran while one was open for 18% of the time, Pallas kernels for 0%

commit v1 on v0

v1 whole, which is shorter than its diff:
```python
import math

import jax
import jax.numpy as jnp
from jax import lax
from jax.sharding import PartitionSpec as P

HEADS = 16
KV_HEADS = 2
HEAD_DIM = 128


epsilon = 1e-06


def attend_all(query, key_cache, value_cache, new_keys, new_values, lengths):
    steps, row_count, _ = query.shape
    group_size = HEADS // KV_HEADS
    queries = query.reshape(steps, row_count, KV_HEADS, group_size, HEAD_DIM)
    queries = jnp.transpose(queries, (1, 2, 0, 3, 4)).reshape(
        row_count, KV_HEADS, steps * group_size, HEAD_DIM
    )
    keys = jnp.concatenate([key_cache, jnp.transpose(new_keys, (1, 0, 2))], axis=1)
    values = jnp.concatenate([value_cache, jnp.transpose(new_values, (1, 0, 2))], axis=1)
    slots = key_cache.shape[1]
    total = keys.shape[1]
    keys = keys.reshape(row_count, total, KV_HEADS, HEAD_DIM)
    values = values.reshape(row_count, total, KV_HEADS, HEAD_DIM)
    scores = jnp.einsum(
        "rgqd,rcgd->rgqc", queries, keys, preferred_element_type=jnp.float32
    ) * (1.0 / math.sqrt(HEAD_DIM))
    slot = jnp.arange(total, dtype=jnp.int32)[None, None, :]
    step = (jnp.arange(steps * group_size, dtype=jnp.int32) // group_size)[None, :, None]
    live = jnp.where(slot < slots, slot < lengths[:, None, None], slot - slots <= step)
    scores = jnp.where(live[:, None], scores, -1e30)
    highest = jnp.max(scores, axis=-1, keepdims=True)
    grown = jnp.exp(scores - highest)
    probs = (grown / jnp.sum(grown, axis=-1, keepdims=True)).astype(jnp.bfloat16)
    attended = jnp.einsum("rgqc,rcgd->rgqd", probs, values, preferred_element_type=jnp.float32)
    attended = attended.reshape(row_count, KV_HEADS, steps, group_size * HEAD_DIM)
    return jnp.transpose(attended, (2, 0, 1, 3)).reshape(steps, row_count, HEADS * HEAD_DIM)


def body(
    residual,
    query,
    new_keys,
    new_values,
    key_cache,
    value_cache,
    lengths,
    norm_gain,
    expert_ids,
    gate_scores,
    learner_gate,
    learner_up,
    learner_down,
):
    axes = ("node", "local")
    steps, row_count, width = residual.shape
    expert_total = learner_gate.shape[0]
    gate_w, up_w, down_w = (
        lax.all_to_all(w.astype(jnp.bfloat16), axes, split_axis=0, concat_axis=1, tiled=True)
        for w in (learner_gate, learner_up, learner_down)
    )
    attended = attend_all(query, key_cache, value_cache, new_keys, new_values, lengths)
    hidden = residual.astype(jnp.float32) + attended
    mean_square = jnp.mean(hidden * hidden, axis=-1, keepdims=True)
    normed = (hidden * lax.rsqrt(mean_square + epsilon) * norm_gain).astype(jnp.bfloat16)
    weights = gate_scores / jnp.sum(gate_scores, axis=-1, keepdims=True)
    chosen = expert_ids[..., None] == jnp.arange(expert_total, dtype=jnp.int32)
    dense = jnp.sum(jnp.where(chosen, weights[..., None], 0.0), axis=2)
    dense = dense.reshape(steps * row_count, expert_total)
    rows = lax.all_gather(normed.reshape(steps * row_count, width), axes, axis=0, tiled=True)
    owned = gate_w.shape[0]
    shares = lax.all_to_all(dense, axes, split_axis=1, concat_axis=0, tiled=True)
    total = None
    for j in range(owned):
        gate_part = jnp.dot(rows, gate_w[j], preferred_element_type=jnp.float32)
        up_part = jnp.dot(rows, up_w[j], preferred_element_type=jnp.float32)
        active = (jax.nn.silu(gate_part) * up_part).astype(jnp.bfloat16)
        served = lax.dot_general(
            active, down_w[j], (((1,), (1,)), ((), ())), preferred_element_type=jnp.float32
        )
        served = served * shares[:, j : j + 1]
        total = served if total is None else total + served
    summed = lax.psum_scatter(total.astype(jnp.bfloat16), axes, scatter_dimension=0, tiled=True)
    mixture_sum = summed.astype(jnp.float32).reshape(residual.shape)
    return (mixture_sum.astype(jnp.bfloat16), (hidden + mixture_sum).astype(jnp.bfloat16))


def solution(mesh):
    return jax.shard_map(
        body,
        mesh=mesh,
        in_specs=(
            P(None, ("groups", "node", "local"), None),
            P(None, ("groups", "node", "local"), None),
            P(None, ("groups", "node", "local"), None),
            P(None, ("groups", "node", "local"), None),
            P(("groups", "node", "local"), None, None),
            P(("groups", "node", "local"), None, None),
            P(("groups", "node", "local")),
            P(),
            P(None, ("groups", "node", "local"), None),
            P(None, ("groups", "node", "local"), None),
            P(None, ("node", "local"), None),
            P(None, ("node", "local"), None),
            P(None, ("node", "local"), None),
        ),
        out_specs=(
            P(None, ("groups", "node", "local"), None),
            P(None, ("groups", "node", "local"), None),
        ),
        check_vma=False,
    )
```

time: 393 us -> 266 us (0.68)
  waiting for transfers between devices: 259 us -> 190 us
  starting transfers between devices: 48.3 us -> 22.4 us
  matrix products: 40.2 us -> 16.8 us
  local copies, waits for them, and re-layouts: 21 us -> 5.78 us
  between operations: 1.42 us -> 14.2 us
  other arithmetic: 21.2 us -> 16.8 us
    all_to_all x11 -> x4, waiting for transfers between devices: 259 us -> 118 us  [the longest x3 118 us: body(): lax.all_to_all(w.astype(jnp.bfloat16), axes, split_axis=0, concat_axis=1,...]
    reduce_scatter x0 -> x1, waiting for transfers between devices: none -> 71.3 us  [body(): lax.psum_scatter(total.astype(jnp.bfloat16), axes, scatter_dimension=0, t...]
    all_to_all x11 -> x4, starting transfers between devices: 48.3 us -> 22.3 us  [the longest x3 15 us: body(): lax.all_to_all(w.astype(jnp.bfloat16), axes, split_axis=0, concat_axis=1,...]
    dot_general x28 -> x4, matrix products: 40.2 us -> 16.8 us  [the longest x1 8.8 us: body(): lax.dot_general(active, down_w[j], (((1,), (1,)), ((), ())), preferred_el...]
    gather x4 -> x0, local copies, waits for them, and re-layouts: 7.48 us -> none  [body(): picked = flat_rows[slot_map]]
    reduce_sum x25 -> x3, other arithmetic: 6.95 us -> 1.09 us  [the longest x1 0.74 us: body(): weights = gate_scores / jnp.sum(gate_scores, axis=-1, keepdims=True)]
    convert_element_type x6 -> x5, other arithmetic: 9.98 us -> 12.5 us  [the longest x3 9.98 us: body(): w.astype(jnp.bfloat16)]
  transfers between devices with their start and end apart: 11 -> 6, of which waited for: 11 -> 4; matrix products, arithmetic and copies ran while one was open for 18% -> 10% of each run, Pallas kernels for 0% -> 0%
where the time goes in v1:
time: 266 us
  waiting for transfers between devices  190 us (71%)
  starting transfers between devices  22.4 us (8%)
  other arithmetic  16.8 us (6%)
  matrix products  16.8 us (6%)
  between operations  14.2 us (5%)
  local copies, waits for them, and re-layouts  5.78 us (2%)
    all_to_all x3, waiting for transfers between devices, body(): lax.all_to_all(w.astype(jnp.bfloat16), axes, split_axis=0, concat_axis=1,...  118 us
    reduce_scatter x1, waiting for transfers between devices, body(): lax.psum_scatter(total.astype(jnp.bfloat16), axes, scatter_dimension=0, t...  71.3 us
    all_to_all x3, starting transfers between devices, body(): lax.all_to_all(w.astype(jnp.bfloat16), axes, split_axis=0, concat_axis=1,...  15 us
    convert_element_type x3, other arithmetic, body(): w.astype(jnp.bfloat16)  9.98 us
    dot_general x1, matrix products, body(): lax.dot_general(active, down_w[j], (((1,), (1,)), ((), ())), preferred_el...  8.8 us
    all_to_all x1, starting transfers between devices, body(): lax.all_to_all(dense, axes, split_axis=1, concat_axis=0, tiled=True)  7.36 us
    dot_general x1, matrix products, body(): gate_part = jnp.dot(rows, gate_w[j], preferred_element_type=jnp.float32)  5.7 us
  transfers between devices with their start and end apart: 6, of which 4 were waited for; matrix products, arithmetic and copies ran while one was open for 10% of the time, Pallas kernels for 0%

profile of v1, /device:TPU:0, one launch (start us, length us, event | category | flops | bytes accessed | tf_op | source)
XLA Modules:
  0.0 265.6 jit_solution(2010481402164367677)
XLA Ops:
  7.2 0.7 reduce_sum.38
  7.9 0.7 broadcast_divide_fusion
  8.6 0.1 copy.50
  8.7 0.8 copy.49
  9.5 0.2 select_reduce_fusion
  9.7 0.7 copy.51
  10.4 7.4 %all-to-all-start.3 = ((f32[64,16,1]{0,2,1:T(1,128)}), f32[64,16,1]{0,2,1:T(1,128)S(1)}, u32[]{:S(2)}, u32[]{:S(2)}) async-start(f32[64,16,1]{0,2,1:T(1,128)} %copy.51), calls=%async_computation.3 | async-start | bytes 16384 | tf_op jit(solution)/shard_map/all_to_all | solution.py:76
  17.8 0.7 iota_compare_fusion.1
  18.5 0.8 copy.68
  19.3 0.8 copy.67
  20.1 0.0 copy-start.1
  20.1 1.1 copy.56
  21.1 1.1 pad_maximum_fusion.1
  22.3 0.2 reshape.150
  22.5 0.0 copy-done.1
  22.6 0.1 pad_maximum_fusion
  22.6 0.2 reshape.149
  22.9 0.1 broadcast_compare_fusion
  23.0 0.5 fusion.4
  23.5 0.4 fusion.13
  23.9 1.9 fusion.5
  25.7 0.0 copy-start
  25.7 0.2 reshape.144
  25.9 0.4 copy.48
  26.3 0.5 reshape.145
  26.8 0.0 copy-done
  26.8 0.1 multiply_reduce_fusion
  26.9 3.3 %convert_element_type.32 = bf16[16,128,384]{2,1,0:T(8,128)(2,1)} convert(f32[16,128,384]{2,1,0:T(8,128)} %param.23) | non-fusion elementwise | flops 786432 | bytes 4718592 | tf_op jit(solution)/shard_map/convert_element_type | solution.py:63
  30.3 0.0 all-to-all-done.3
  30.3 6.1 %all-to-all-start = ((bf16[16,128,384]{2,1,0:T(8,128)(2,1)}), bf16[16,128,384]{2,1,0:T(8,128)(2,1)S(1)}, u32[]{:S(2)}, u32[]{:S(2)}) async-start(bf16[16,128,384]{2,1,0:T(8,128)(2,1)} %convert_element_type.32), calls=%async_computation | async-start | bytes 3145728 | tf_op jit(solution)/shard_map/all_to_all | solution.py:63
  36.4 0.0 all-gather.2.cloned.1.call-start
  36.5 0.0 copy-done.2
  36.5 0.8 multiply_convert_fusion.2
  37.3 0.0 all-gather.2.cloned.1.call-update
  37.3 3.3 %convert_element_type.33 = bf16[16,128,384]{2,1,0:T(8,128)(2,1)} convert(f32[16,128,384]{2,1,0:T(8,128)} %param.24) | non-fusion elementwise | flops 786432 | bytes 4718592 | tf_op jit(solution)/shard_map/convert_element_type | solution.py:63
  40.7 42.4 %all-to-all-done = bf16[16,128,384]{2,1,0:T(8,128)(2,1)S(1)} async-done(((bf16[16,128,384]{2,1,0:T(8,128)(2,1)}), bf16[16,128,384]{2,1,0:T(8,128)(2,1)S(1)}, u32[]{:S(2)}, u32[]{:S(2)}) %all-to-all-start) | async-done | bytes 1572896 | tf_op jit(solution)/shard_map/all_to_all | solution.py:63
  83.1 4.4 %all-to-all-start.1 = ((bf16[16,128,384]{2,1,0:T(8,128)(2,1)}), bf16[16,128,384]{2,1,0:T(8,128)(2,1)}, u32[]{:S(2)}, u32[]{:S(2)}) async-start(bf16[16,128,384]{2,1,0:T(8,128)(2,1)} %convert_element_type.33), calls=%async_computation.1 | async-start | bytes 3145728 | tf_op jit(solution)/shard_map/all_to_all | solution.py:63
  87.5 3.3 %convert_element_type.35 = bf16[16,128,384]{2,1,0:T(8,128)(2,1)} convert(f32[16,128,384]{2,1,0:T(8,128)} %param.25) | non-fusion elementwise | flops 786432 | bytes 4718592 | tf_op jit(solution)/shard_map/convert_element_type | solution.py:63
  90.8 43.4 %all-to-all-done.1 = bf16[16,128,384]{2,1,0:T(8,128)(2,1)} async-done(((bf16[16,128,384]{2,1,0:T(8,128)(2,1)}), bf16[16,128,384]{2,1,0:T(8,128)(2,1)}, u32[]{:S(2)}, u32[]{:S(2)}) %all-to-all-start.1) | async-done | bytes 1572896 | tf_op jit(solution)/shard_map/all_to_all | solution.py:63
  134.2 4.4 %all-to-all-start.2 = ((bf16[16,128,384]{2,1,0:T(8,128)(2,1)}), bf16[16,128,384]{2,1,0:T(8,128)(2,1)}, u32[]{:S(2)}, u32[]{:S(2)}) async-start(bf16[16,128,384]{2,1,0:T(8,128)(2,1)} %convert_element_type.35), calls=%async_computation.2 | async-start | bytes 3145728 | tf_op jit(solution)/shard_map/all_to_all | solution.py:63
  138.6 0.0 reduce-scatter.2.cloned.1.call-start
  138.7 0.1 mul.55
  138.8 5.7 %fusion.14 = f32[1024,384]{1,0:T(8,128)} fusion(bf16[1024,2048]{1,0:T(8,128)(2,1)} %all-gather.2.cloned.1.call-done, bf16[2048,384]{1,0:T(8,128)(2,1)S(1)} %bitcast.38), kind=kOutput, calls=%fused_computation.40 | convolution fusion | flops 1610612736 | bytes 7340032 | tf_op jit(solution)/shard_map/dot_general | solution.py:79
  144.5 32.4 %all-to-all-done.2 = bf16[16,128,384]{2,1,0:T(8,128)(2,1)} async-done(((bf16[16,128,384]{2,1,0:T(8,128)(2,1)}), bf16[16,128,384]{2,1,0:T(8,128)(2,1)}, u32[]{:S(2)}, u32[]{:S(2)}) %all-to-all-start.2) | async-done | bytes 1572896 | tf_op jit(solution)/shard_map/all_to_all | solution.py:63
  176.8 8.8 %multiply_convert_fusion = bf16[1024,2048]{1,0:T(8,128)(2,1)} fusion(bf16[2048,384]{1,0:T(8,128)(2,1)} %bitcast.9, f32[1024]{0:T(1024)S(1)} %mul.55, f32[1024,384]{1,0:T(8,128)} %fusion.14, bf16[1024,2048]{1,0:T(8,128)(2,1)} %all-gather.2.cloned.1.call-done, bf16[2048,384]{1,0:T(8,128)(2,1)} %bitcast.8), kind=kOutput, calls=%fused_computation.1 | convolution fusion | flops 3227779072 | bytes 13111296 | tf_op jit(solution)/shard_map/dot_general | solution.py:82
  185.6 0.0 reduce-scatter.2.cloned.1.call-update
  185.7 71.3 %reduce-scatter.2.cloned.1.call-done = bf16[64,2048]{1,0:T(8,128)(2,1)} async-done(((bf16[1024,2048]{1,0:T(8,128)(2,1)}), bf16[64,2048]{1,0:T(8,128)(2,1)}) %reduce-scatter.2.cloned.1.call-update) | async-done | bytes 262160 | tf_op jit(solution)/shard_map/reduce_scatter | solution.py:87
  257.0 1.8 add_convert_fusion
  (8 shorter events, 0.1 us)
Async XLA Ops:
  10.4 19.9 %all-to-all-start.3 = ((f32[64,16,1]{0,2,1:T(1,128)}), f32[64,16,1]{0,2,1:T(1,128)S(1)}, u32[]{:S(2)}, u32[]{:S(2)}) async-start(f32[64,16,1]{0,2,1:T(1,128)} %copy.51), calls=%async_computation.3 | async-start | bytes 16384 | tf_op jit(solution)/shard_map/all_to_all | solution.py:76
  20.1 2.5 copy-start.1
  25.7 1.1 copy-start
  30.3 6.2 %copy-start.2 = (f32[2048]{0:T(1024)S(1)}, f32[2048]{0:T(1024)}, u32[]{:S(2)}) copy-start(f32[2048]{0:T(1024)} %param.20) | copy-start | bytes 24580
  30.3 52.8 %all-to-all-start = ((bf16[16,128,384]{2,1,0:T(8,128)(2,1)}), bf16[16,128,384]{2,1,0:T(8,128)(2,1)S(1)}, u32[]{:S(2)}, u32[]{:S(2)}) async-start(bf16[16,128,384]{2,1,0:T(8,128)(2,1)} %convert_element_type.32), calls=%async_computation | async-start | bytes 3145728 | tf_op jit(solution)/shard_map/all_to_all | solution.py:63
  36.4 102.4 %all-gather.2.cloned.1.call-start = ((), (), s32[]{:S(2)}) async-start(), calls=%async_computation.5 | async-start | bytes 4456448 | tf_op jit(solution)/shard_map/all_gather | solution.py:74
  83.1 51.1 %all-to-all-start.1 = ((bf16[16,128,384]{2,1,0:T(8,128)(2,1)}), bf16[16,128,384]{2,1,0:T(8,128)(2,1)}, u32[]{:S(2)}, u32[]{:S(2)}) async-start(bf16[16,128,384]{2,1,0:T(8,128)(2,1)} %convert_element_type.33), calls=%async_computation.1 | async-start | bytes 3145728 | tf_op jit(solution)/shard_map/all_to_all | solution.py:63
  134.2 42.6 %all-to-all-start.2 = ((bf16[16,128,384]{2,1,0:T(8,128)(2,1)}), bf16[16,128,384]{2,1,0:T(8,128)(2,1)}, u32[]{:S(2)}, u32[]{:S(2)}) async-start(bf16[16,128,384]{2,1,0:T(8,128)(2,1)} %convert_element_type.35), calls=%async_computation.2 | async-start | bytes 3145728 | tf_op jit(solution)/shard_map/all_to_all | solution.py:63
  138.6 118.3 %reduce-scatter.2.cloned.1.call-start = ((), (), s32[]{:S(2)}) async-start(), calls=%async_computation.6 | async-start | bytes 4456448 | tf_op jit(solution)/shard_map/reduce_scatter | solution.py:87
Sparse Core Ops, SparseCore 0:
  40.0 84.3 all-gather.1
  185.8 71.1 reduce-scatter.1

commit v2 on v1

--- a/solution.py
+++ b/solution.py
@@ -1,8 +1,11 @@
+import functools
 import math
 
 import jax
 import jax.numpy as jnp
 from jax import lax
+from jax.experimental import pallas as pl
+from jax.experimental.pallas import tpu as pltpu
 from jax.sharding import PartitionSpec as P
 
 HEADS = 16
@@ -41,7 +44,302 @@
     return jnp.transpose(attended, (2, 0, 1, 3)).reshape(steps, row_count, HEADS * HEAD_DIM)
 
 
+MESH = pl.DeviceIdType.MESH
+
+
+def flip_low(v):
+    return v + 1 - 2 * lax.rem(v, 2)
+
+
+def flip_high(v):
+    return v + 2 - 4 * (v // 2)
+
+
+def flip(v, bits):
+    v = flip_low(v) if bits % 2 else v
+    return flip_high(v) if bits >= 2 else v
+
+
+CROSS = [(dn, dl) for dl in (2, 3) for dn in (0, 1, 2, 3)]
+SAME = [(dn, dl) for dl in (0, 1) for dn in (0, 1, 2, 3)]
+
+
+def moe_kernel(
+    normed, share, lg, lu, ld, out,
+    stage_x, stage_s, send_x, send_s, wbuf, rows, part, rbuf, shares,
+    load_x, load_s, xs, xr, ss, sr, fs, fr, hs, hr, ags, agr, rss, rsr,
+):
+    g, n, l = lax.axis_index("groups"), lax.axis_index("node"), lax.axis_index("local")
+    me = n * 4 + l
+    core, x = lax.rem(n, 2), n // 2
+    block = core * 8 + x * 4 + lax.rem(l, 2) * 2 + l // 2
+    steps, held, width = normed.shape
+    depth = lg.shape[1]
+    half = depth // 2
+    mine = pl.ds(pl.multiple_of(g * half, half), half)
+
+    def peer(dn, dl):
+        return flip(n, dn), flip(l, dl)
+
+    def to(dn, dl):
+        pn, plo = peer(dn, dl)
+        return (g, pn, plo)
+
+    learners = (lg, lu, ld)
+
+    def loads(i, cross):
+        dn, dl = (CROSS if cross else SAME)[i]
+        pn, plo = peer(dn, dl)
+        p = pn * 4 + plo
+        made = []
+        for a, ref in enumerate(learners):
+            if cross:
+                made.append(pltpu.make_async_copy(ref.at[p, mine], stage_x.at[i, a], load_x.at[i, a]))
+            else:
+                made.append(pltpu.make_async_copy(ref.at[p], stage_s.at[i, a], load_s.at[i, a]))
+        return made
+
+    for i in range(8):
+        for c in loads(i, True):
+            c.start()
+    for i in range(8):
+        for c in loads(i, False):
+            c.start()
+
+    barrier = pltpu.get_barrier_semaphore()
+    everyone = [to(dn, dl) for dn, dl in CROSS + SAME[1:]] + [(1 - g, n, l)]
+    for who in everyone:
+        pl.semaphore_signal(barrier, inc=1, device_id=who, device_id_type=MESH)
+    for t in range(steps):
+        rows[t, block] = normed[t]
+    shares[me] = share[me]
+    pl.semaphore_wait(barrier, len(everyone))
+
+    HOPS = ((0, 2), (0, 1), (2, 0), (1, 0))
+
+    def gather(k, t):
+        size = 1 << k
+        base = block // size * size
+        ref = rows.at[t, pl.ds(base, size)]
+        return pltpu.make_async_remote_copy(
+            src_ref=ref, dst_ref=ref, send_sem=ags.at[k, t], recv_sem=agr.at[k, t],
+            device_id=to(*HOPS[k]), device_id_type=MESH,
+        )
+
+    OFFSET = (14, 12, 8, 0)
+
+    def scatter(k, t):
+        size = 1 << k
+        mybase = block // size * size
+        base = mybase + size - 2 * size * lax.rem(block // size, 2)
+        return pltpu.make_async_remote_copy(
+            src_ref=part.at[t, pl.ds(base, size)], dst_ref=rbuf.at[t, pl.ds(OFFSET[k], size)],
+            send_sem=rss.at[k, t], recv_sem=rsr.at[k, t],
+            device_id=to(*HOPS[k]), device_id_type=MESH,
+        )
+
+    def share_copy(i):
+        dn, dl = (CROSS + SAME)[i]
+        pn, plo = peer(dn, dl)
+        return pltpu.make_async_remote_copy(
+            src_ref=share.at[pn * 4 + plo], dst_ref=shares.at[me], send_sem=hs.at[i], recv_sem=hr.at[i],
+            device_id=(g, pn, plo), device_id_type=MESH,
+        )
+
+    def cross_copy(i):
+        return pltpu.make_async_remote_copy(
+            src_ref=send_x.at[i], dst_ref=wbuf.at[:, me, mine], send_sem=xs.at[i], recv_sem=xr.at[i],
+            device_id=to(*CROSS[i]), device_id_type=MESH,
+        )
+
+    def same_copy(i):
+        return pltpu.make_async_remote_copy(
+            src_ref=send_s.at[i], dst_ref=wbuf.at[:, me], send_sem=ss.at[i], recv_sem=sr.at[i],
+            device_id=to(*SAME[i]), device_id_type=MESH,
+        )
+
+    def forward(i):
+        pn, plo = peer(*CROSS[i])
+        ref = wbuf.at[:, pn * 4 + plo, mine]
+        return pltpu.make_async_remote_copy(
+            src_ref=ref, dst_ref=ref, send_sem=fs.at[i], recv_sem=fr.at[i],
+            device_id=(1 - g, n, l), device_id_type=MESH,
+        )
+
+    for t in range(steps):
+        gather(0, t).start()
+    for i in range(16):
+        if i != 8:
+            share_copy(i).start()
+    for i in range(8):
+        for c in loads(i, True):
+            c.wait()
+        send_x[i] = stage_x[i].astype(jnp.bfloat16)
+        cross_copy(i).start()
+    for i in range(1, 8):
+        for c in loads(i, False):
+            c.wait()
+        send_s[i] = stage_s[i].astype(jnp.bfloat16)
+        same_copy(i).start()
+    for c in loads(0, False):
+        c.wait()
+    wbuf[:, me] = stage_s[0].astype(jnp.bfloat16)
+
+    for t in range(steps):
+        gather(0, t).wait_recv()
+        gather(1, t).start()
+    for i in range(4):
+        cross_copy(i).wait_recv()
+        forward(i).start()
+    for t in range(steps):
+        gather(1, t).wait_recv()
+        gather(2, t).start()
+    for i in range(4, 8):
+        cross_copy(i).wait_recv()
+        forward(i).start()
+    for t in range(steps):
+        gather(2, t).wait_recv()
+        gather(3, t).start()
+    for i in range(16):
+        if i != 8:
+            share_copy(i).wait_recv()
+    for i in range(1, 8):
+        same_copy(i).wait_recv()
+    for i in range(8):
+        forward(i).wait_recv()
+    for t in range(steps):
+        gather(3, t).wait_recv()
+
+    count = 16 * held
+    hidden_units = lg.shape[2]
+    eye = lax.broadcasted_iota(jnp.int32, (held, 128), 0)
+    lane = lax.broadcasted_iota(jnp.int32, (held, 128), 1)
+
+    def compute(t):
+        tokens = rows[t].reshape(count, width)
+        gate_part = jnp.dot(tokens, wbuf[0].reshape(width, hidden_units), preferred_element_type=jnp.float32)
+        up_part = jnp.dot(tokens, wbuf[1].reshape(width, hidden_units), preferred_element_type=jnp.float32)
+        active = (gate_part / (1.0 + jnp.exp(-gate_part)) * up_part).astype(jnp.bfloat16)
+        columns = []
+        for b in range(16):
+            bc, bx, bl = b // 8, b // 4 % 2, (b // 2 % 2) + 2 * (b % 2)
+            source = (bx * 2 + bc) * 4 + bl
+            line = shares[source, 0:1, :]
+            picked = jnp.where(lane == eye + t * held, line, 0.0)
+            columns.append(jnp.sum(picked, axis=1, keepdims=True))
+        column = jnp.concatenate(columns, axis=0)
+        for j in range(4):
+            wide = width // 4
+            down = wbuf[2, 4 * j : 4 * j + 4].reshape(wide, hidden_units)
+            served = lax.dot_general(
+                active, down, (((1,), (1,)), ((), ())), preferred_element_type=jnp.float32
+            )
+            part[t, :, :, wide * j : wide * (j + 1)] = (
+                (served * column).astype(jnp.bfloat16).reshape(16, held, wide)
+            )
+
+    def reduce(k, t):
+        size = 1 << k
+        base = block // size * size
+        scatter(k, t).wait_recv()
+        total = part[t, pl.ds(base, size)].astype(jnp.float32) + rbuf[
+            t, OFFSET[k] : OFFSET[k] + size
+        ].astype(jnp.float32)
+        if k == 0:
+            out[t] = total[0]
+        else:
+            part[t, pl.ds(base, size)] = total.astype(jnp.bfloat16)
+            scatter(k - 1, t).start()
+
+    def turn(t, carry):
+        compute(t)
+        scatter(3, t).start()
+
+        @pl.when(t >= 1)
+        def _():
+            reduce(3, t - 1)
+
+        return carry
+
+    lax.fori_loop(0, steps, turn, 0)
+    reduce(3, steps - 1)
+    for k in (2, 1, 0):
+        for t in range(steps):
+            reduce(k, t)
+
+    for t in range(steps):
+        for k in range(4):
+            gather(k, t).wait_send()
+            scatter(k, t).wait_send()
+    for i in range(16):
+        if i != 8:
+            share_copy(i).wait_send()
+    for i in range(8):
+        cross_copy(i).wait_send()
+        forward(i).wait_send()
+    for i in range(1, 8):
+        same_copy(i).wait_send()
+
+
+def kernel_call(normed, share, lg, lu, ld):
+    steps, held, width = normed.shape
+    experts, depth, units = lg.shape
+    bf16, f32 = jnp.bfloat16, jnp.float32
+    vmem = pl.BlockSpec(memory_space=pltpu.VMEM)
+    hbm = pl.BlockSpec(memory_space=pl.ANY)
+    dma = pltpu.SemaphoreType.DMA
+    return pl.pallas_call(
+        moe_kernel,
+        out_shape=jax.ShapeDtypeStruct((steps, held, width), f32),
+        in_specs=[vmem, vmem, hbm, hbm, hbm],
+        out_specs=vmem,
+        scratch_shapes=[
+            pltpu.VMEM((8, 3, depth // 2, units), f32),
+            pltpu.VMEM((8, 3, depth, units), f32),
+            pltpu.VMEM((8, 3, depth // 2, units), bf16),
+            pltpu.VMEM((8, 3, depth, units), bf16),
+            pltpu.VMEM((3, 16, depth, units), bf16),
+            pltpu.VMEM((steps, 16, held, width), bf16),
+            pltpu.VMEM((steps, 16, held, width), bf16),
+            pltpu.VMEM((steps, 15, held, width), bf16),
+            pltpu.VMEM((16, 8, 128), f32),
+            dma((8, 3)), dma((8, 3)),
+            dma((8,)), dma((8,)), dma((8,)), dma((8,)), dma((8,)), dma((8,)),
+            dma((16,)), dma((16,)),
+            dma((4, steps)), dma((4, steps)), dma((4, steps)), dma((4, steps)),
+        ],
+        compiler_params=pltpu.CompilerParams(
+            collective_id=0, has_side_effects=True, vmem_limit_bytes=56 * 1024 * 1024
+        ),
+    )(normed, share, lg, lu, ld)
+
+
+def plain_mix(normed, dense, learner_gate, learner_up, learner_down):
+    axes = ("node", "local")
+    steps, row_count, width = normed.shape
+    gate_w, up_w, down_w = (
+        lax.all_to_all(w.astype(jnp.bfloat16), axes, split_axis=0, concat_axis=1, tiled=True)
+        for w in (learner_gate, learner_up, learner_down)
+    )
+    rows = lax.all_gather(normed.reshape(steps * row_count, width), axes, axis=0, tiled=True)
+    owned = gate_w.shape[0]
+    shares = lax.all_to_all(dense, axes, split_axis=1, concat_axis=0, tiled=True)
+    total = None
+    for j in range(owned):
+        gate_part = jnp.dot(rows, gate_w[j], preferred_element_type=jnp.float32)
+        up_part = jnp.dot(rows, up_w[j], preferred_element_type=jnp.float32)
+        active = (jax.nn.silu(gate_part) * up_part).astype(jnp.bfloat16)
+        served = lax.dot_general(
+            active, down_w[j], (((1,), (1,)), ((), ())), preferred_element_type=jnp.float32
+        )
+        served = served * shares[:, j : j + 1]
+        total = served if total is None else total + served
+    summed = lax.psum_scatter(total.astype(jnp.bfloat16), axes, scatter_dimension=0, tiled=True)
+    return summed.astype(jnp.float32).reshape(normed.shape)
+
+
 def body(
+    fused,
     residual,
     query,
     new_keys,
@@ -56,13 +354,8 @@
     learner_up,
     learner_down,
 ):
-    axes = ("node", "local")
     steps, row_count, width = residual.shape
     expert_total = learner_gate.shape[0]
-    gate_w, up_w, down_w = (
-        lax.all_to_all(w.astype(jnp.bfloat16), axes, split_axis=0, concat_axis=1, tiled=True)
-        for w in (learner_gate, learner_up, learner_down)
-    )
     attended = attend_all(query, key_cache, value_cache, new_keys, new_values, lengths)
     hidden = residual.astype(jnp.float32) + attended
     mean_square = jnp.mean(hidden * hidden, axis=-1, keepdims=True)
@@ -71,27 +364,20 @@
     chosen = expert_ids[..., None] == jnp.arange(expert_total, dtype=jnp.int32)
     dense = jnp.sum(jnp.where(chosen, weights[..., None], 0.0), axis=2)
     dense = dense.reshape(steps * row_count, expert_total)
-    rows = lax.all_gather(normed.reshape(steps * row_count, width), axes, axis=0, tiled=True)
-    owned = gate_w.shape[0]
-    shares = lax.all_to_all(dense, axes, split_axis=1, concat_axis=0, tiled=True)
-    total = None
-    for j in range(owned):
-        gate_part = jnp.dot(rows, gate_w[j], preferred_element_type=jnp.float32)
-        up_part = jnp.dot(rows, up_w[j], preferred_element_type=jnp.float32)
-        active = (jax.nn.silu(gate_part) * up_part).astype(jnp.bfloat16)
-        served = lax.dot_general(
-            active, down_w[j], (((1,), (1,)), ((), ())), preferred_element_type=jnp.float32
-        )
-        served = served * shares[:, j : j + 1]
-        total = served if total is None else total + served
-    summed = lax.psum_scatter(total.astype(jnp.bfloat16), axes, scatter_dimension=0, tiled=True)
-    mixture_sum = summed.astype(jnp.float32).reshape(residual.shape)
+    if fused:
+        share = jnp.pad(dense.T, ((0, 0), (0, 128 - steps * row_count)))
+        share = jnp.broadcast_to(share[:, None, :], (expert_total, 8, 128))
+        mixture_sum = kernel_call(normed, share, learner_gate, learner_up, learner_down)
+    else:
+        mixture_sum = plain_mix(normed, dense, learner_gate, learner_up, learner_down)
     return (mixture_sum.astype(jnp.bfloat16), (hidden + mixture_sum).astype(jnp.bfloat16))
 
 
 def solution(mesh):
+    sizes = dict(mesh.shape)
+    fused = sizes == {"groups": 2, "node": 4, "local": 4}
     return jax.shard_map(
-        body,
+        functools.partial(body, fused),
         mesh=mesh,
         in_specs=(
             P(None, ("groups", "node", "local"), None),

time: 266 us -> 153 us (0.58)
  waiting for transfers between devices: 190 us -> 0 us
  Pallas kernels: 0 us -> 141 us
  starting transfers between devices: 22.4 us -> 0 us
  matrix products: 16.8 us -> 2.34 us
  between operations: 14.2 us -> 0.84 us
  other arithmetic: 16.8 us -> 5.1 us
    pallas_call x0 -> x1, Pallas kernels: none -> 141 us  [kernel_call(): pl.pallas_call(moe_kernel, out_shape=jax.ShapeDtypeStruct((steps, held, w...]
    all_to_all x4 -> x0, waiting for transfers between devices: 118 us -> none  [the longest x3 118 us: body(): lax.all_to_all(w.astype(jnp.bfloat16), axes, split_axis=0, concat_axis=1,...]
    reduce_scatter x1 -> x0, waiting for transfers between devices: 71.3 us -> none  [body(): lax.psum_scatter(total.astype(jnp.bfloat16), axes, scatter_dimension=0, t...]
    all_to_all x4 -> x0, starting transfers between devices: 22.3 us -> none  [the longest x3 15 us: body(): lax.all_to_all(w.astype(jnp.bfloat16), axes, split_axis=0, concat_axis=1,...]
    dot_general x2 -> x0, matrix products: 14.5 us -> none  [the longest x1 8.8 us: body(): lax.dot_general(active, down_w[j], (((1,), (1,)), ((), ())), preferred_el...]
    convert_element_type x3 -> x0, other arithmetic: 9.98 us -> none  [body(): w.astype(jnp.bfloat16)]
  transfers between devices with their start and end apart: 6 -> 0, of which waited for: 4 -> 0; matrix products, arithmetic and copies ran while one was open for 10% -> 0% of each run, Pallas kernels for 0% -> 0%
where the time goes in v2:
time: 153 us
  Pallas kernels  141 us (92%)
  other arithmetic  5.1 us (3%)
  local copies, waits for them, and re-layouts  3.3 us (2%)
  matrix products  2.34 us (2%)
    pallas_call x1, Pallas kernels, kernel_call(): pl.pallas_call(moe_kernel, out_shape=jax.ShapeDtypeStruct((steps, held, w...  141 us

profile of v2, /device:TPU:0, one launch (start us, length us, event | category | flops | bytes accessed | tf_op | source)
XLA Modules:
  0.0 152.6 jit_solution(11000481128966888980)
XLA Ops:
  0.6 0.0 copy-start.2
  0.6 0.8 copy.60
  1.5 0.0 copy-start.7
  1.5 1.1 pad_maximum_fusion
  2.6 0.2 reshape.124
  2.9 0.0 copy-done.2
  2.9 0.0 copy-start.4
  2.9 0.0 copy-start.1
  3.0 0.1 broadcast_compare_fusion
  3.0 0.0 copy-done.7
  3.0 0.1 iota_compare_fusion.1
  3.2 0.5 fusion.4
  3.6 0.4 fusion.12
  4.0 0.0 copy-done.4
  4.1 0.0 copy-done.1
  4.1 0.1 pad_maximum_fusion.1
  4.1 0.2 reshape.125
  4.4 1.9 %fusion.5 = f32[16,2,32,128]{3,2,1,0:T(8,128)S(1)} fusion(bf16[16,84,2,128]{3,2,1,0:T(2,128)(2,1)S(1)} %reshape.125, f32[16,2,32]{2,1,0:T(2,128)S(1)} %fusion.12, f32[16,2,32,84]{3,2,1,0:T(8,128)S(1)} %fusion.4), kind=kOutput, calls=%fused_computation.8 | convolution fusion | flops 22279252 | bytes 1560576 | tf_op jit(solution)/shard_map/rgqc,rcgd->rgqd/dot_general | solution.py:42
  6.2 0.0 copy-start
  6.2 0.2 reshape.121
  6.4 0.0 copy-start.6
  6.4 0.4 copy.58
  6.9 0.0 copy-start.3
  6.9 0.0 copy-start.5
  6.9 0.5 reshape.122
  7.3 0.0 copy-done
  7.4 0.1 multiply_reduce_fusion
  7.5 0.0 copy-done.6
  7.5 0.8 multiply_convert_fusion.normed
  8.3 0.0 copy-done.3
  8.4 0.1 copy.40
  8.5 0.0 copy-done.5
  8.5 0.1 copy.39
  8.5 0.2 select_reduce_fusion
  8.8 0.1 copy.41
  8.8 0.6 broadcast_in_dim.73.share
  9.5 141.0 %shard_map.140 = f32[4,16,2048]{2,1,0:T(8,128)} custom-call(bf16[4,16,2048]{2,1,0:T(8,128)(2,1)} %multiply_convert_fusion.normed, f32[16,8,128]{2,1,0:T(8,128)} %broadcast_in_dim.73.share, f32[16,128,384]{2,1,0:T(8,128)} %lg.1, f32[16,128,384]{2,1,0:T(8,128)} %lu.1, f32[16,128,384]{2,1,0:T(8,128)} %ld.1), custom_call_target="tpu_custom_call" | custom-call | tf_op jit(solution)/shard_map/pallas_call | solution.py:291
  150.5 2.1 %add_convert_fusion = (bf16[4,16,2048]{2,1,0:T(8,128)(2,1)}, bf16[4,16,2048]{2,1,0:T(8,128)(2,1)}) fusion(f32[4,16,2048]{2,1,0:T(8,128)} %shard_map.140, f32[4,16,2048]{2,1,0:T(8,128)S(1)} %reshape.122, bf16[4,16,2048]{2,1,0:T(8,128)(2,1)S(1)} %copy-done), kind=kLoop, calls=%fused_computation.12 | loop fusion | flops 655360 | bytes 1835008 | tf_op jit(solution)/shard_map/convert_element_type | solution.py:373
  (10 shorter events, 0.2 us)
Async XLA Ops:
  0.6 2.2 %copy-start.2 = (bf16[4,16,2048]{2,1,0:T(8,128)(2,1)S(1)}, bf16[4,16,2048]{2,1,0:T(8,128)(2,1)}, u32[]{:S(2)}) copy-start(bf16[4,16,2048]{2,1,0:T(8,128)(2,1)} %param.14) | copy-start | bytes 786436
  1.5 1.6 %copy-start.7 = (s32[16]{0:T(128)S(1)}, s32[16]{0:T(128)}, u32[]{:S(2)}) copy-start(s32[16]{0:T(128)} %param.19) | copy-start | bytes 196
  2.9 1.2 copy-start.4
  2.9 1.2 copy-start.1
  6.2 1.1 copy-start
  6.4 1.1 copy-start.6
  6.9 1.5 copy-start.3
  6.9 1.6 %copy-start.5 = (s32[4,16,8]{1,2,0:T(8,128)S(1)}, s32[4,16,8]{1,2,0:T(8,128)}, u32[]{:S(2)}) copy-start(s32[4,16,8]{1,2,0:T(8,128)} %param.21) | copy-start | bytes 6148

commit v3 on v2

--- a/solution.py
+++ b/solution.py
@@ -60,8 +60,9 @@
     return flip_high(v) if bits >= 2 else v
 
 
-CROSS = [(dn, dl) for dl in (2, 3) for dn in (0, 1, 2, 3)]
-SAME = [(dn, dl) for dl in (0, 1) for dn in (0, 1, 2, 3)]
+CROSS = [(dn, dl) for dl in (2, 3, 1) for dn in (0, 1, 2, 3)]
+SAME = [(dn, 0) for dn in (0, 1, 2, 3)]
+FAR, NEAR = len(CROSS), len(SAME)
 
 
 def moe_kernel(
@@ -99,10 +100,10 @@
                 made.append(pltpu.make_async_copy(ref.at[p], stage_s.at[i, a], load_s.at[i, a]))
         return made
 
-    for i in range(8):
+    for i in range(FAR):
         for c in loads(i, True):
             c.start()
-    for i in range(8):
+    for i in range(NEAR):
         for c in loads(i, False):
             c.start()
 
@@ -169,14 +170,33 @@
     for t in range(steps):
         gather(0, t).start()
     for i in range(16):
-        if i != 8:
+        if i != FAR:
             share_copy(i).start()
-    for i in range(8):
-        for c in loads(i, True):
-            c.wait()
-        send_x[i] = stage_x[i].astype(jnp.bfloat16)
-        cross_copy(i).start()
-    for i in range(1, 8):
+    def send_cross(lo, hi):
+        for i in range(lo, hi):
+            for c in loads(i, True):
+                c.wait()
+            send_x[i] = stage_x[i].astype(jnp.bfloat16)
+            cross_copy(i).start()
+
+    def pass_on(lo, hi):
+        for i in range(lo, hi):
+            cross_copy(i).wait_recv()
+            forward(i).start()
+
+    def next_hop(k):
+        for t in range(steps):
+            gather(k, t).wait_recv()
+            gather(k + 1, t).start()
+
+    send_cross(0, 4)
+    next_hop(0)
+    send_cross(4, 8)
+    next_hop(1)
+    send_cross(8, 12)
+    pass_on(0, 4)
+    next_hop(2)
+    for i in range(1, NEAR):
         for c in loads(i, False):
             c.wait()
         send_s[i] = stage_s[i].astype(jnp.bfloat16)
@@ -184,28 +204,13 @@
     for c in loads(0, False):
         c.wait()
     wbuf[:, me] = stage_s[0].astype(jnp.bfloat16)
-
-    for t in range(steps):
-        gather(0, t).wait_recv()
-        gather(1, t).start()
-    for i in range(4):
-        cross_copy(i).wait_recv()
-        forward(i).start()
-    for t in range(steps):
-        gather(1, t).wait_recv()
-        gather(2, t).start()
-    for i in range(4, 8):
-        cross_copy(i).wait_recv()
-        forward(i).start()
-    for t in range(steps):
-        gather(2, t).wait_recv()
-        gather(3, t).start()
+    pass_on(4, FAR)
     for i in range(16):
-        if i != 8:
+        if i != FAR:
             share_copy(i).wait_recv()
-    for i in range(1, 8):
+    for i in range(1, NEAR):
         same_copy(i).wait_recv()
-    for i in range(8):
+    for i in range(FAR):
         forward(i).wait_recv()
     for t in range(steps):
         gather(3, t).wait_recv()
@@ -272,12 +277,12 @@
             gather(k, t).wait_send()
             scatter(k, t).wait_send()
     for i in range(16):
-        if i != 8:
+        if i != FAR:
             share_copy(i).wait_send()
-    for i in range(8):
+    for i in range(FAR):
         cross_copy(i).wait_send()
         forward(i).wait_send()
-    for i in range(1, 8):
+    for i in range(1, NEAR):
         same_copy(i).wait_send()
 
 
@@ -294,17 +299,17 @@
         in_specs=[vmem, vmem, hbm, hbm, hbm],
         out_specs=vmem,
         scratch_shapes=[
-            pltpu.VMEM((8, 3, depth // 2, units), f32),
-            pltpu.VMEM((8, 3, depth, units), f32),
-            pltpu.VMEM((8, 3, depth // 2, units), bf16),
-            pltpu.VMEM((8, 3, depth, units), bf16),
+            pltpu.VMEM((FAR, 3, depth // 2, units), f32),
+            pltpu.VMEM((NEAR, 3, depth, units), f32),
+            pltpu.VMEM((FAR, 3, depth // 2, units), bf16),
+            pltpu.VMEM((NEAR, 3, depth, units), bf16),
             pltpu.VMEM((3, 16, depth, units), bf16),
             pltpu.VMEM((steps, 16, held, width), bf16),
             pltpu.VMEM((steps, 16, held, width), bf16),
             pltpu.VMEM((steps, 15, held, width), bf16),
             pltpu.VMEM((16, 8, 128), f32),
-            dma((8, 3)), dma((8, 3)),
-            dma((8,)), dma((8,)), dma((8,)), dma((8,)), dma((8,)), dma((8,)),
+            dma((FAR, 3)), dma((NEAR, 3)),
+            dma((FAR,)), dma((FAR,)), dma((NEAR,)), dma((NEAR,)), dma((FAR,)), dma((FAR,)),
             dma((16,)), dma((16,)),
             dma((4, steps)), dma((4, steps)), dma((4, steps)), dma((4, steps)),
         ],

time: 153 us -> 157 us (1.026)
  Pallas kernels: 141 us -> 146 us
    pallas_call x1, Pallas kernels: 141 us -> 146 us  [kernel_call(): pl.pallas_call(moe_kernel, out_shape=jax.ShapeDtypeStruct((steps, held, w...]
where the time goes in v3:
time: 157 us
  Pallas kernels  146 us (93%)
  other arithmetic  5.1 us (3%)
  local copies, waits for them, and re-layouts  3.3 us (2%)
  matrix products  2.34 us (1%)
    pallas_call x1, Pallas kernels, kernel_call(): pl.pallas_call(moe_kernel, out_shape=jax.ShapeDtypeStruct((steps, held, w...  146 us

profile of v3, /device:TPU:0, one launch (start us, length us, event | category | flops | bytes accessed | tf_op | source)
XLA Modules:
  0.0 157.2 jit_solution(12904628453638831417)
XLA Ops:
  0.6 0.0 copy-start.2
  0.6 0.8 copy.60
  1.5 0.0 copy-start.7
  1.5 1.1 pad_maximum_fusion
  2.6 0.2 reshape.124
  2.9 0.0 copy-done.2
  2.9 0.0 copy-start.4
  2.9 0.0 copy-start.1
  3.0 0.1 broadcast_compare_fusion
  3.0 0.0 copy-done.7
  3.0 0.1 iota_compare_fusion.1
  3.2 0.5 fusion.4
  3.6 0.4 fusion.12
  4.0 0.0 copy-done.4
  4.1 0.0 copy-done.1
  4.1 0.1 pad_maximum_fusion.1
  4.1 0.2 reshape.125
  4.4 1.9 %fusion.5 = f32[16,2,32,128]{3,2,1,0:T(8,128)S(1)} fusion(bf16[16,84,2,128]{3,2,1,0:T(2,128)(2,1)S(1)} %reshape.125, f32[16,2,32]{2,1,0:T(2,128)S(1)} %fusion.12, f32[16,2,32,84]{3,2,1,0:T(8,128)S(1)} %fusion.4), kind=kOutput, calls=%fused_computation.8 | convolution fusion | flops 22279252 | bytes 1560576 | tf_op jit(solution)/shard_map/rgqc,rcgd->rgqd/dot_general | solution.py:42
  6.2 0.0 copy-start
  6.2 0.2 reshape.121
  6.4 0.0 copy-start.6
  6.4 0.4 copy.58
  6.9 0.0 copy-start.3
  6.9 0.0 copy-start.5
  6.9 0.5 reshape.122
  7.3 0.0 copy-done
  7.4 0.1 multiply_reduce_fusion
  7.5 0.0 copy-done.6
  7.5 0.8 multiply_convert_fusion.normed
  8.3 0.0 copy-done.3
  8.4 0.1 copy.40
  8.5 0.0 copy-done.5
  8.5 0.1 copy.39
  8.5 0.2 select_reduce_fusion
  8.8 0.1 copy.41
  8.8 0.6 broadcast_in_dim.73.share
  9.5 145.6 %shard_map.140 = f32[4,16,2048]{2,1,0:T(8,128)} custom-call(bf16[4,16,2048]{2,1,0:T(8,128)(2,1)} %multiply_convert_fusion.normed, f32[16,8,128]{2,1,0:T(8,128)} %broadcast_in_dim.73.share, f32[16,128,384]{2,1,0:T(8,128)} %lg.1, f32[16,128,384]{2,1,0:T(8,128)} %lu.1, f32[16,128,384]{2,1,0:T(8,128)} %ld.1), custom_call_target="tpu_custom_call" | custom-call | tf_op jit(solution)/shard_map/pallas_call | solution.py:296
  155.1 2.1 %add_convert_fusion = (bf16[4,16,2048]{2,1,0:T(8,128)(2,1)}, bf16[4,16,2048]{2,1,0:T(8,128)(2,1)}) fusion(f32[4,16,2048]{2,1,0:T(8,128)} %shard_map.140, f32[4,16,2048]{2,1,0:T(8,128)S(1)} %reshape.122, bf16[4,16,2048]{2,1,0:T(8,128)(2,1)S(1)} %copy-done), kind=kLoop, calls=%fused_computation.12 | loop fusion | flops 655360 | bytes 1835008 | tf_op jit(solution)/shard_map/convert_element_type | solution.py:378
  (10 shorter events, 0.2 us)
Async XLA Ops:
  0.6 2.2 %copy-start.2 = (bf16[4,16,2048]{2,1,0:T(8,128)(2,1)S(1)}, bf16[4,16,2048]{2,1,0:T(8,128)(2,1)}, u32[]{:S(2)}) copy-start(bf16[4,16,2048]{2,1,0:T(8,128)(2,1)} %param.14) | copy-start | bytes 786436
  1.5 1.6 %copy-start.7 = (s32[16]{0:T(128)S(1)}, s32[16]{0:T(128)}, u32[]{:S(2)}) copy-start(s32[16]{0:T(128)} %param.19) | copy-start | bytes 196
  2.9 1.2 copy-start.4
  2.9 1.2 copy-start.1
  6.2 1.1 copy-start
  6.4 1.1 copy-start.6
  6.9 1.5 copy-start.3
  6.9 1.6 %copy-start.5 = (s32[4,16,8]{1,2,0:T(8,128)S(1)}, s32[4,16,8]{1,2,0:T(8,128)}, u32[]{:S(2)}) copy-start(s32[4,16,8]{1,2,0:T(8,128)} %param.21) | copy-start | bytes 6148

commit v4 on v2

--- a/solution.py
+++ b/solution.py
@@ -185,21 +185,16 @@
         c.wait()
     wbuf[:, me] = stage_s[0].astype(jnp.bfloat16)
 
-    for t in range(steps):
-        gather(0, t).wait_recv()
-        gather(1, t).start()
-    for i in range(4):
-        cross_copy(i).wait_recv()
-        forward(i).start()
-    for t in range(steps):
-        gather(1, t).wait_recv()
-        gather(2, t).start()
-    for i in range(4, 8):
-        cross_copy(i).wait_recv()
-        forward(i).start()
-    for t in range(steps):
-        gather(2, t).wait_recv()
-        gather(3, t).start()
+    for wave in range(steps + 2):
+        for k in range(3):
+            t = wave - k
+            if 0 <= t < steps:
+                gather(k, t).wait_recv()
+                gather(k + 1, t).start()
+        if wave >= 2:
+            for i in (2 * wave - 4, 2 * wave - 3):
+                cross_copy(i).wait_recv()
+                forward(i).start()
     for i in range(16):
         if i != 8:
             share_copy(i).wait_recv()
@@ -263,9 +258,11 @@
 
     lax.fori_loop(0, steps, turn, 0)
     reduce(3, steps - 1)
-    for k in (2, 1, 0):
-        for t in range(steps):
-            reduce(k, t)
+    for wave in range(steps + 2):
+        for k in (2, 1, 0):
+            t = wave - 2 + k
+            if 0 <= t < steps:
+                reduce(k, t)
 
     for t in range(steps):
         for k in range(4):

time: 153 us -> 158 us (1.033)
  Pallas kernels: 141 us -> 146 us
    pallas_call x1, Pallas kernels: 141 us -> 146 us  [kernel_call(): pl.pallas_call(moe_kernel, out_shape=jax.ShapeDtypeStruct((steps, held, w...]
where the time goes in v4:
time: 158 us; the launch traced here: 157 us
  Pallas kernels  146 us (92%)
  other arithmetic  5.1 us (3%)
  local copies, waits for them, and re-layouts  3.3 us (2%)
  matrix products  2.34 us (1%)
    pallas_call x1, Pallas kernels, kernel_call(): pl.pallas_call(moe_kernel, out_shape=jax.ShapeDtypeStruct((steps, held, w...  146 us

profile of v4, /device:TPU:0, one launch (start us, length us, event | category | flops | bytes accessed | tf_op | source)
XLA Modules:
  0.0 157.4 jit_solution(5851896190072211354)
XLA Ops:
  0.6 0.0 copy-start.2
  0.6 0.8 copy.60
  1.5 0.0 copy-start.7
  1.5 1.1 pad_maximum_fusion
  2.6 0.2 reshape.124
  2.9 0.0 copy-done.2
  2.9 0.0 copy-start.4
  2.9 0.0 copy-start.1
  3.0 0.1 broadcast_compare_fusion
  3.0 0.0 copy-done.7
  3.0 0.1 iota_compare_fusion.1
  3.2 0.5 fusion.4
  3.6 0.4 fusion.12
  4.0 0.0 copy-done.4
  4.1 0.0 copy-done.1
  4.1 0.1 pad_maximum_fusion.1
  4.1 0.2 reshape.125
  4.4 1.9 %fusion.5 = f32[16,2,32,128]{3,2,1,0:T(8,128)S(1)} fusion(bf16[16,84,2,128]{3,2,1,0:T(2,128)(2,1)S(1)} %reshape.125, f32[16,2,32]{2,1,0:T(2,128)S(1)} %fusion.12, f32[16,2,32,84]{3,2,1,0:T(8,128)S(1)} %fusion.4), kind=kOutput, calls=%fused_computation.8 | convolution fusion | flops 22279252 | bytes 1560576 | tf_op jit(solution)/shard_map/rgqc,rcgd->rgqd/dot_general | solution.py:42
  6.2 0.0 copy-start
  6.2 0.2 reshape.121
  6.4 0.0 copy-start.6
  6.4 0.4 copy.58
  6.9 0.0 copy-start.3
  6.9 0.0 copy-start.5
  6.9 0.5 reshape.122
  7.3 0.0 copy-done
  7.4 0.1 multiply_reduce_fusion
  7.5 0.0 copy-done.6
  7.5 0.8 multiply_convert_fusion.normed
  8.3 0.0 copy-done.3
  8.4 0.1 copy.40
  8.5 0.0 copy-done.5
  8.5 0.1 copy.39
  8.5 0.2 select_reduce_fusion
  8.8 0.1 copy.41
  8.8 0.6 broadcast_in_dim.73.share
  9.5 145.8 %shard_map.140 = f32[4,16,2048]{2,1,0:T(8,128)} custom-call(bf16[4,16,2048]{2,1,0:T(8,128)(2,1)} %multiply_convert_fusion.normed, f32[16,8,128]{2,1,0:T(8,128)} %broadcast_in_dim.73.share, f32[16,128,384]{2,1,0:T(8,128)} %lg.1, f32[16,128,384]{2,1,0:T(8,128)} %lu.1, f32[16,128,384]{2,1,0:T(8,128)} %ld.1), custom_call_target="tpu_custom_call" | custom-call | tf_op jit(solution)/shard_map/pallas_call | solution.py:288
  155.3 2.1 %add_convert_fusion = (bf16[4,16,2048]{2,1,0:T(8,128)(2,1)}, bf16[4,16,2048]{2,1,0:T(8,128)(2,1)}) fusion(f32[4,16,2048]{2,1,0:T(8,128)} %shard_map.140, f32[4,16,2048]{2,1,0:T(8,128)S(1)} %reshape.122, bf16[4,16,2048]{2,1,0:T(8,128)(2,1)S(1)} %copy-done), kind=kLoop, calls=%fused_computation.12 | loop fusion | flops 655360 | bytes 1835008 | tf_op jit(solution)/shard_map/convert_element_type | solution.py:370
  (10 shorter events, 0.2 us)
Async XLA Ops:
  0.6 2.2 %copy-start.2 = (bf16[4,16,2048]{2,1,0:T(8,128)(2,1)S(1)}, bf16[4,16,2048]{2,1,0:T(8,128)(2,1)}, u32[]{:S(2)}) copy-start(bf16[4,16,2048]{2,1,0:T(8,128)(2,1)} %param.14) | copy-start | bytes 786436
  1.5 1.6 %copy-start.7 = (s32[16]{0:T(128)S(1)}, s32[16]{0:T(128)}, u32[]{:S(2)}) copy-start(s32[16]{0:T(128)} %param.19) | copy-start | bytes 196
  2.9 1.2 copy-start.4
  2.9 1.2 copy-start.1
  6.2 1.1 copy-start
  6.4 1.1 copy-start.6
  6.9 1.5 copy-start.3
  6.9 1.6 %copy-start.5 = (s32[4,16,8]{1,2,0:T(8,128)S(1)}, s32[4,16,8]{1,2,0:T(8,128)}, u32[]{:S(2)}) copy-start(s32[4,16,8]{1,2,0:T(8,128)} %param.21) | copy-start | bytes 6148
